TPU v7x, 128 devices: a whole 4x4x4 slice. The times are simulated.
128 devices in a mesh: dp: 4 (over y_hi, core), mp: 32 (over z, y_lo, x).
Axes of the slice: x: 4, y: 4 (y_hi: 2, y_lo: 2; y = y_hi * 2 + y_lo), z: 4, core: 2. Of those that a mesh axis runs over, the one named last changes fastest.
Arguments:
- pooled: bfloat16 [16384, 6144], P('dp', 'mp'), may hold values from -6 to 6
- proj: bfloat16 [6144, 1024], replicated, may hold values from -0.078125 to 0.078125
- text: bfloat16 [16384, 1024], P(('dp', 'mp')), may hold values from -0.1875 to 0.1875
- logit_scale: float32 [1], replicated, may hold values from 8 to 16
- logit_bias: float32 [1], replicated, may hold values from -6 to -4
Outputs:
- grad_text: float32 [16384, 1024], P(('dp', 'mp'))
- grad_proj: float32 [6144, 1024], P('mp')
All inputs are finite; a program needn't handle non-finite values.
Results may differ from a plain program's by a relative error of at most 0.009.
Values may be sent and summed in bfloat16 or wider, within the bound.
A program may use at most 192 MiB of HBM per device.

v0:
```python
import jax
import jax.numpy as jnp
from jax import lax
from jax.sharding import PartitionSpec as P

EPS = 1e-06


def from_behind(value, axis, steps):
    count = lax.axis_size(axis)
    pairs = [(source, (source + steps) % count) for source in range(count)]
    return lax.ppermute(value, axis, pairs)


def unit_rows(values):
    inverse = lax.rsqrt(jnp.sum(values * values, axis=-1, keepdims=True) + EPS)
    return ((values * inverse).astype(jnp.bfloat16), inverse)


def on_device(pooled, proj, text, logit_scale, logit_bias):
    rows = text.shape[0]
    embed = proj.shape[1]
    groups = lax.axis_size("dp")
    shards = lax.axis_size("mp")
    group = rows * shards
    dp_index = lax.axis_index("dp")
    mp_index = lax.axis_index("mp")
    full_rows = lax.all_to_all(pooled, "mp", split_axis=0, concat_axis=1, tiled=True)
    projected = jnp.dot(full_rows, proj, preferred_element_type=jnp.float32)
    own_unit, own_inverse = unit_rows(projected)
    text_unit, text_inverse = unit_rows(text.astype(jnp.float32))
    image_unit = lax.all_gather(own_unit, "mp", axis=0, tiled=True)
    image_ids = dp_index * group + jnp.arange(group, dtype=jnp.int32)
    span = text_unit
    span_first = mp_index * rows
    span_rows = span.shape[0]
    span_offsets = span_first + jnp.arange(span_rows, dtype=jnp.int32)
    scale = logit_scale[0]
    bias = logit_bias[0]
    contract = (((0,), (0,)), ((), ()))
    image_grad = jnp.zeros((image_unit.shape[0], embed), jnp.float32)
    carried = jnp.zeros((span_rows, embed), jnp.float32)
    for step in range(groups):
        source = (dp_index - step) % groups
        logits = scale * jnp.dot(image_unit, span.T, preferred_element_type=jnp.float32) + bias
        match = image_ids[:, None] == (source * group + span_offsets)[None, :]
        sign = jnp.where(match, jnp.float32(1.0), jnp.float32(-1.0))
        weights = (-sign * jax.nn.sigmoid(-sign * logits)).astype(jnp.bfloat16)
        image_grad = image_grad + scale * jnp.dot(weights, span, preferred_element_type=jnp.float32)
        contrib = scale * lax.dot_general(
            weights, image_unit, contract, preferred_element_type=jnp.float32
        )
        carried = from_behind(carried + contrib, "dp", 1)
        if step + 1 < groups:
            span = from_behind(span, "dp", 1)
    own_grad = lax.psum_scatter(image_grad, "mp", scatter_dimension=0, tiled=True)
    text_float = text_unit.astype(jnp.float32)
    grad_text = (
        carried - text_float * jnp.sum(text_float * carried, axis=-1, keepdims=True)
    ) * text_inverse
    own_float = own_unit.astype(jnp.float32)
    delta = (
        (own_grad - own_float * jnp.sum(own_float * own_grad, axis=-1, keepdims=True)) * own_inverse
    ).astype(jnp.bfloat16)
    partial_grad = lax.dot_general(
        pooled,
        lax.all_gather(delta, "mp", axis=0, tiled=True),
        contract,
        preferred_element_type=jnp.float32,
    )
    grad_proj = lax.psum(partial_grad, "dp")
    return (grad_text, grad_proj)


def solution(mesh):
    return jax.shard_map(
        on_device,
        mesh=mesh,
        in_specs=(P("dp", "mp"), P(), P(("dp", "mp"), None), P(), P()),
        out_specs=(P(("dp", "mp"), None), P("mp", None)),
        check_vma=False,
    )
```

profile of v0, /device:TPU:1, one launch (start us, length us, event | category | flops | bytes accessed | tf_op | source)
XLA Modules:
  0.0 713.0 jit_solution(15158780674032412960)
XLA Ops:
  9.0 30.6 %all_to_all.19 = bf16[32,128,192]{1,2,0:T(8,128)(2,1)S(1)} all-to-all(bf16[32,128,192]{1,2,0:T(8,128)(2,1)S(1)} %copy_bitcast_fusion), channel_id=1, replica_groups=mesh['dp'=4,'mp'=32] {'mp'}, dimensions={0} | all-to-all | bytes 3145728 | tf_op jit(solution)/shard_map/all_to_all | solution.py:28
  39.6 6.5 multiply_reduce_fusion
  47.3 5.3 collective-permute-start.1
  61.2 10.0 %collective-permute-done.3 = bf16[128,1024]{1,0:T(8,128)(2,1)} collective-permute-done((bf16[128,1024]{1,0:T(8,128)(2,1)S(1)}, bf16[128,1024]{1,0:T(8,128)(2,1)}, u32[]{:S(2)}, u32[]{:S(2)}) %collective-permute-start.3) | collective-permute-done | bytes 262176 | tf_op jit(solution)/shard_map/ppermute | solution.py:12
  71.2 4.1 collective-permute-start.5
  75.3 120.0 %all-gather.3.cloned.1.call-done = bf16[4096,1024]{1,0:T(8,128)(2,1)} async-done(((bf16[128,1024]{1,0:T(8,128)(2,1)}), bf16[4096,1024]{1,0:T(8,128)(2,1)}) %all-gather.3.cloned.1.call-update) | async-done | bytes 8388624 | tf_op jit(solution)/shard_map/all_gather | solution.py:32
  195.3 4.9 fusion.31
  200.3 8.4 %fusion.46 = f32[4096,1024]{1,0:T(8,128)} fusion(bf16[4096,128]{1,0:T(8,128)(2,1)S(1)} %fusion.31, bf16[128,1024]{1,0:T(8,128)(2,1)S(1)} %fusion.34), kind=kOutput, calls=%fused_computation.69 | convolution fusion | flops 1073741824 | bytes 18087936 | tf_op jit(solution)/shard_map/dot_general | solution.py:49
  212.6 8.1 %fusion.47 = f32[4096,1024]{1,0:T(8,128)} fusion(bf16[4096,128]{1,0:T(8,128)(2,1)S(1)} %fusion.28, bf16[128,1024]{1,0:T(8,128)(2,1)S(1)} %copy-done.9), kind=kOutput, calls=%fused_computation.70 | convolution fusion | flops 1073741824 | bytes 18087936 | tf_op jit(solution)/shard_map/dot_general | solution.py:49
  224.6 9.2 %fusion.48 = f32[4096,1024]{1,0:T(8,128)} fusion(bf16[4096,128]{1,0:T(8,128)(2,1)S(1)} %fusion.25, bf16[128,1024]{1,0:T(8,128)(2,1)} %collective-permute-done.3), kind=kOutput, calls=%fused_computation.71 | convolution fusion | flops 1073741824 | bytes 18087936 | tf_op jit(solution)/shard_map/dot_general | solution.py:49
  238.7 23.0 %add_multiply_fusion = f32[4096,1024]{1,0:T(8,128)} fusion(f32[4096,1024]{1,0:T(8,128)} %fusion.48, f32[4096,1024]{1,0:T(8,128)} %fusion.46, f32[4096,1024]{1,0:T(8,128)} %fusion.47, bf16[4096,128]{1,0:T(8,128)(2,1)S(1)} %fusion.22, bf16[128,1024]{1,0:T(8,128)(2,1)} %collective-permute-done.5, f32[]{:T(128)} %bitcast.42), kind=kOutput, calls=%fused_computation | convolution fusion | flops 1090519040 | bytes 68419584 | tf_op jit(solution)/shard_map/dot_general | solution.py:49
  261.8 204.6 %reduce-scatter.2.cloned.1.call-done = f32[128,1024]{1,0:T(8,128)} async-done(((f32[4096,1024]{1,0:T(8,128)}), f32[128,1024]{1,0:T(8,128)}) %reduce-scatter.2.cloned.1.call-update) | async-done | bytes 524304 | tf_op jit(solution)/shard_map/reduce_scatter | solution.py:56
  469.8 5.1 convolution_multiply_fusion.7
  474.9 21.3 %collective-permute-start = (f32[128,1024]{1,0:T(8,128)S(1)}, f32[128,1024]{1,0:T(8,128)S(1)}, u32[]{:S(2)}, u32[]{:S(2)}) collective-permute-start(f32[128,1024]{1,0:T(8,128)S(1)} %convolution_multiply_fusion.7), channel_id=1, source_target_pairs={{0,32},{32,64},{64,96},{96,0},{1,33},{33,65},{65,97},{97,1},{2,34}... | collective-permute-start | bytes 1572872 | tf_op jit(solution)/shard_map/ppermute | solution.py:12
  496.3 18.0 %collective-permute-done = f32[128,1024]{1,0:T(8,128)S(1)} collective-permute-done((f32[128,1024]{1,0:T(8,128)S(1)}, f32[128,1024]{1,0:T(8,128)S(1)}, u32[]{:S(2)}, u32[]{:S(2)}) %collective-permute-start) | collective-permute-done | bytes 524320 | tf_op jit(solution)/shard_map/ppermute | solution.py:12
  514.3 4.9 fusion.32
  519.2 5.4 collective-permute-start.2
  525.9 14.6 %collective-permute-done.2 = f32[128,1024]{1,0:T(8,128)S(1)} collective-permute-done((f32[128,1024]{1,0:T(8,128)S(1)}, f32[128,1024]{1,0:T(8,128)S(1)}, u32[]{:S(2)}, u32[]{:S(2)}) %collective-permute-start.2) | collective-permute-done | bytes 524320 | tf_op jit(solution)/shard_map/ppermute | solution.py:12
  540.6 5.8 collective-permute-start.4
  547.8 12.9 %collective-permute-done.4 = f32[128,1024]{1,0:T(8,128)S(1)} collective-permute-done((f32[128,1024]{1,0:T(8,128)S(1)}, f32[128,1024]{1,0:T(8,128)S(1)}, u32[]{:S(2)}, u32[]{:S(2)}) %collective-permute-start.4) | collective-permute-done | bytes 524320 | tf_op jit(solution)/shard_map/ppermute | solution.py:12
  560.7 4.4 collective-permute-start.6
  565.1 68.0 %all-gather.5.cloned.1.call-done = bf16[4096,1024]{1,0:T(8,128)(2,1)} async-done(((bf16[128,1024]{1,0:T(8,128)(2,1)}), bf16[4096,1024]{1,0:T(8,128)(2,1)}) %all-gather.5.cloned.1.call-update) | async-done | bytes 8388624 | tf_op jit(solution)/shard_map/all_gather | solution.py:67
  633.1 6.1 convolution_bitcast_fusion
  640.4 63.9 %all-reduce.2.cloned.1.call-done = f32[192,1024]{1,0:T(8,128)} async-done(((f32[192,1024]{1,0:T(8,128)}), f32[192,1024]{1,0:T(8,128)}) %all-reduce.2.cloned.1.call-update) | async-done | bytes 786448 | tf_op jit(solution)/shard_map/psum | solution.py:71
  (60 shorter events, 32.6 us)
Async XLA Ops:
  7.2 1.4 copy-start
  7.2 188.1 %all-gather.3.cloned.1.call-start = ((), (), s32[]{:S(2)}) async-start(), calls=%async_computation.2 | async-start | bytes 8650752 | tf_op jit(solution)/shard_map/all_gather | solution.py:32
  39.6 7.4 %copy-start.7 = (bf16[128,1024]{1,0:T(8,128)(2,1)S(1)}, bf16[128,1024]{1,0:T(8,128)(2,1)}, u32[]{:S(2)}) copy-start(bf16[128,1024]{1,0:T(8,128)(2,1)} %param.7) | copy-start | bytes 786436
  46.9 419.4 %reduce-scatter.2.cloned.1.call-start = ((), (), s32[]{:S(2)}) async-start(), calls=%async_computation.3 | async-start | bytes 17301504 | tf_op jit(solution)/shard_map/reduce_scatter | solution.py:56
  47.3 8.6 %collective-permute-start.1 = (bf16[128,1024]{1,0:T(8,128)(2,1)S(1)}, bf16[128,1024]{1,0:T(8,128)(2,1)S(1)}, u32[]{:S(2)}, u32[]{:S(2)}) collective-permute-start(bf16[128,1024]{1,0:T(8,128)(2,1)S(1)} %fusion.34), channel_id=1, source_target_pairs={{0,32},{32,64},{64,96},{96,0},{1,33},{33,65},{65,97},{97,1},{2,34}... | collective-permute-start | bytes 786440 | tf_op jit(solution)/shard_map/ppermute | solution.py:12
  55.9 144.4 %copy-start.8 = (bf16[128,1024]{1,0:T(8,128)(2,1)}, bf16[128,1024]{1,0:T(8,128)(2,1)S(1)}, u32[]{:S(2)}) copy-start(bf16[128,1024]{1,0:T(8,128)(2,1)S(1)} %collective-permute-done.1) | copy-start | bytes 786436
  55.9 15.3 %collective-permute-start.3 = (bf16[128,1024]{1,0:T(8,128)(2,1)S(1)}, bf16[128,1024]{1,0:T(8,128)(2,1)}, u32[]{:S(2)}, u32[]{:S(2)}) collective-permute-start(bf16[128,1024]{1,0:T(8,128)(2,1)S(1)} %collective-permute-done.1), channel_id=1, source_target_pairs={{0,32},{32,64},{64,96},{96,0},{1,33},{33,65},{65,97},{97,1},{2,34}... | collective-permute-start | bytes 786440 | tf_op jit(solution)/shard_map/ppermute | solution.py:12
  71.2 162.6 %collective-permute-start.5 = (bf16[128,1024]{1,0:T(8,128)(2,1)}, bf16[128,1024]{1,0:T(8,128)(2,1)}, u32[]{:S(2)}, u32[]{:S(2)}) collective-permute-start(bf16[128,1024]{1,0:T(8,128)(2,1)} %collective-permute-done.3), channel_id=1, source_target_pairs={{0,32},{32,64},{64,96},{96,0},{1,33},{33,65},{65,97},{97,1},{2,34}... | collective-permute-start | bytes 786440 | tf_op jit(solution)/shard_map/ppermute | solution.py:12
  200.3 8.4 %copy-start.4 = (bf16[4096,128]{1,0:T(8,128)(2,1)}, bf16[4096,128]{1,0:T(8,128)(2,1)S(1)}, u32[]{:S(2)}) copy-start(bf16[4096,128]{1,0:T(8,128)(2,1)S(1)} %fusion.31) | copy-start | bytes 3145732
  200.3 8.4 %copy-start.1 = (bf16[4096,1024]{1,0:T(8,128)(2,1)S(1)}, bf16[4096,1024]{1,0:T(8,128)(2,1)}, u32[]{:S(2)}) copy-start(bf16[4096,1024]{1,0:T(8,128)(2,1)} %all-gather.3.cloned.1.call-done) | copy-start | bytes 25165828
  208.7 4.0 copy-start.9
  224.6 9.2 %copy-start.2 = (bf16[4096,128]{1,0:T(8,128)(2,1)}, bf16[4096,128]{1,0:T(8,128)(2,1)S(1)}, u32[]{:S(2)}) copy-start(bf16[4096,128]{1,0:T(8,128)(2,1)S(1)} %fusion.25) | copy-start | bytes 3145732
  237.7 1.0 copy-start.5
  261.7 371.4 %all-gather.5.cloned.1.call-start = ((), (), s32[]{:S(2)}) async-start(), calls=%async_computation.4 | async-start | bytes 8650752 | tf_op jit(solution)/shard_map/all_gather | solution.py:67
  469.5 234.8 %all-reduce.2.cloned.1.call-start = ((), (), s32[]{:S(2)}) async-start(), calls=%async_computation.5 | async-start | bytes 1572864 | tf_op jit(solution)/shard_map/psum | solution.py:71
  469.8 54.8 %slice-start = ((s8[8388608]{0:T(1024)(128)(4,1)}), s8[4194304]{0:T(1024)(128)(4,1)S(1)}, s32[]{:S(2)}) async-start(s8[8388608]{0:T(1024)(128)(4,1)} %bitcast.53), calls=%async_computation.6 | async-start | bytes 8388608
  474.9 39.3 %collective-permute-start = (f32[128,1024]{1,0:T(8,128)S(1)}, f32[128,1024]{1,0:T(8,128)S(1)}, u32[]{:S(2)}, u32[]{:S(2)}) collective-permute-start(f32[128,1024]{1,0:T(8,128)S(1)} %convolution_multiply_fusion.7), channel_id=1, source_target_pairs={{0,32},{32,64},{64,96},{96,0},{1,33},{33,65},{65,97},{97,1},{2,34}... | collective-permute-start | bytes 1572872 | tf_op jit(solution)/shard_map/ppermute | solution.py:12
  514.2 10.3 %slice-start.1 = ((s8[8388608]{0:T(1024)(128)(4,1)}), s8[4194304]{0:T(1024)(128)(4,1)S(1)}, s32[]{:S(2)}) async-start(s8[8388608]{0:T(1024)(128)(4,1)} %bitcast.53), calls=%async_computation.7 | async-start | bytes 8388608
  514.2 10.3 %copy-start.3 = (bf16[4096,128]{1,0:T(8,128)(2,1)S(1)}, bf16[4096,128]{1,0:T(8,128)(2,1)}, u32[]{:S(2)}) copy-start(bf16[4096,128]{1,0:T(8,128)(2,1)} %copy-done.2) | copy-start | bytes 3145732
  519.2 21.4 %collective-permute-start.2 = (f32[128,1024]{1,0:T(8,128)S(1)}, f32[128,1024]{1,0:T(8,128)S(1)}, u32[]{:S(2)}, u32[]{:S(2)}) collective-permute-start(f32[128,1024]{1,0:T(8,128)S(1)} %fusion.32), channel_id=1, source_target_pairs={{0,32},{32,64},{64,96},{96,0},{1,33},{33,65},{65,97},{97,1},{2,34}... | collective-permute-start | bytes 1572872 | tf_op jit(solution)/shard_map/ppermute | solution.py:12
  525.9 20.6 %copy-start.6 = (bf16[4096,128]{1,0:T(8,128)(2,1)S(1)}, bf16[4096,128]{1,0:T(8,128)(2,1)}, u32[]{:S(2)}) copy-start(bf16[4096,128]{1,0:T(8,128)(2,1)} %copy-done.5) | copy-start | bytes 3145732
  540.6 20.0 %collective-permute-start.4 = (f32[128,1024]{1,0:T(8,128)S(1)}, f32[128,1024]{1,0:T(8,128)S(1)}, u32[]{:S(2)}, u32[]{:S(2)}) collective-permute-start(f32[128,1024]{1,0:T(8,128)S(1)} %add.176), channel_id=1, source_target_pairs={{0,32},{32,64},{64,96},{96,0},{1,33},{33,65},{65,97},{97,1},{2,34}... | collective-permute-start | bytes 1572872 | tf_op jit(solution)/shard_map/ppermute | solution.py:12
  560.7 78.5 %collective-permute-start.6 = (f32[128,1024]{1,0:T(8,128)S(1)}, f32[128,1024]{1,0:T(8,128)S(1)}, u32[]{:S(2)}, u32[]{:S(2)}) collective-permute-start(f32[128,1024]{1,0:T(8,128)S(1)} %add.182), channel_id=1, source_target_pairs={{0,32},{32,64},{64,96},{96,0},{1,33},{33,65},{65,97},{97,1},{2,34}... | collective-permute-start | bytes 1572872 | tf_op jit(solution)/shard_map/ppermute | solution.py:12
Sparse Core Ops, SparseCore 0:
  47.1 148.1 all-gather.2
  261.9 204.4 reduce-scatter.1
  469.6 163.4 all-gather.4
  639.3 64.9 all-reduce.1
where the time goes:
time: 713 us
  waiting for transfers between devices  515 us (72%)
  matrix products  90.5 us (13%)
  starting transfers between devices  50.7 us (7%)
  blocking collectives  30.6 us (4%)
  between operations  15.3 us (2%)
    reduce_scatter x1, waiting for transfers between devices, on_device(): lax.psum_scatter(image_grad, 'mp', scatter_dimension=0, tiled=True)  205 us
    all_gather x1, waiting for transfers between devices, on_device(): image_unit = lax.all_gather(own_unit, 'mp', axis=0, tiled=True)  120 us
    all_gather x1, waiting for transfers between devices, on_device(): lax.all_gather(delta, 'mp', axis=0, tiled=True)  68 us
    psum x1, waiting for transfers between devices, on_device(): grad_proj = lax.psum(partial_grad, 'dp')  63.9 us
    ppermute x7, waiting for transfers between devices, from_behind(): return lax.ppermute(value, axis, pairs)  58.8 us
    ppermute x7, starting transfers between devices, from_behind(): return lax.ppermute(value, axis, pairs)  50.4 us
    dot_general x4, matrix products, on_device(): jnp.dot(weights, span, preferred_element_type=jnp.float32)  48.6 us
    all_to_all x1, blocking collectives, on_device(): lax.all_to_all(pooled, 'mp', split_axis=0, concat_axis=1, tiled=True)  30.6 us
  transfers between devices with their start and end apart: 11, of which 9 were waited for; matrix products, arithmetic and copies ran while one was open for 8% of the time, Pallas kernels for 0%

commit v1 on v0

v1 whole, which is shorter than its diff:
```python
import functools

import jax
import jax.numpy as jnp
from jax import lax
from jax.experimental import pallas as pl
from jax.experimental.pallas import tpu as pltpu
from jax.sharding import PartitionSpec as P

EPS = 1e-06
LOG2E = 1.4426950408889634
MESH = pl.DeviceIdType.MESH
F32 = jnp.float32
BF16 = jnp.bfloat16
NT = (((1,), (1,)), ((), ()))
TN = (((0,), (0,)), ((), ()))
ROWS = 128
FEATS = 192
EMBED = 1024
HALF = EMBED // 2
MIRROR = [0, 1, 6, 7, 4, 5, 2, 3]
SEND_ORDER = [5, 2, 7, 4, 3, 6, 1]


def sems(*sizes):
    bases, total = [], 0
    for size in sizes:
        bases.append(total)
        total += size
    return bases, total


(S1, S2, TT, TC, IT, IR, DT, XC, XR, GC, GZ, GY, GF), N_SEMS = sems(
    32, 8, 9, 8, 9, 8, 9, 8, 8, 4, 4, 1, 1
)


def kernel(
    pooled_ref, proj_ref, text_ref, scale_ref, bias_ref, gtext_ref, gproj_ref,
    tile, rows_in, proj_v, images, texts, text_acc, img_out, img_in, deltas,
    core_out, core_in, text_out, text_in, gp, gp_out, gp_in, gz_out, gz_in,
    gy_out, gy_in, gf_out, gf_in, weights, send_sem, recv_sem, local_sem, proj_sem,
):
    dp = lax.axis_index("dp")
    mp = lax.axis_index("mp")
    core = dp % 2
    y = (dp // 2) * 2 + (mp // 4) % 2
    x = mp % 4
    z = mp // 8
    y_a = y + 1 - 2 * (y % 2)
    y_b = 3 - y

    def device(x_, y_, z_, core_):
        return ((y_ // 2) * 2 + core_, (z_ * 2 + y_ % 2) * 4 + x_)

    def image_peer(slot):
        return device((x + slot // 2) % 4, y_a if slot % 2 else y, z, core)

    def text_peer(slot):
        return device(x, y_b if slot % 2 else y, (z + slot // 2) % 4, core)

    partner = device(x, y, z, 1 - core)
    across = device(x, (y + 2) % 4, z, core)

    def position(slot):
        return (y_a if slot % 2 else y) % 2 * 4 + (x + slot // 2) % 4

    started = []

    def send(src, dst, sem_out, sem_in, to):
        copy = pltpu.make_async_remote_copy(
            src_ref=src, dst_ref=dst, send_sem=send_sem.at[sem_out],
            recv_sem=recv_sem.at[sem_in], device_id=to, device_id_type=MESH,
        )
        copy.start()
        started.append(copy)

    def arrived(dst, sem):
        pltpu.make_async_copy(dst, dst, recv_sem.at[sem]).wait()

    barrier = pltpu.get_barrier_semaphore()
    peers = [image_peer(s) for s in range(1, 8)] + [text_peer(s) for s in range(1, 8)]
    peers += [partner, across]
    for peer in peers:
        pl.semaphore_signal(barrier, inc=1, device_id=peer, device_id_type=MESH)

    proj_copies = []
    for slot in [MIRROR[s] for s in SEND_ORDER] + [0]:
        for k in range(4):
            shard = (z + k) % 4 * 8 + position(slot)
            copy = pltpu.make_async_copy(
                proj_ref.at[pl.ds(pl.multiple_of(shard * FEATS, FEATS), FEATS), :],
                proj_v.at[slot, pl.ds(k * FEATS, FEATS), :],
                proj_sem.at[slot, k],
            )
            copy.start()
            proj_copies.append((slot, copy))

    def block(ref, slot, rows=ROWS):
        return ref.at[pl.ds(slot * rows, rows), :]

    def part(k, slot):
        return tile.at[pl.ds(k * FEATS, FEATS), pl.ds(slot * ROWS, ROWS)]

    def shard_columns(dz, slot):
        start = (z + dz) % 4 * 1024 + position(slot) * ROWS
        return pooled_ref.at[:, pl.ds(pl.multiple_of(start, ROWS), ROWS)]

    pl.semaphore_wait(barrier, len(peers))

    local = []
    for slot in SEND_ORDER + [0]:
        for dz in (2, 1, 3):
            k = (4 - dz) % 4
            send(shard_columns(dz, slot), part(k, slot), S1 + dz * 8 + slot,
                 S1 + k * 8 + slot, text_peer(2 * dz))
        copy = pltpu.make_async_copy(shard_columns(0, slot), part(0, slot), local_sem.at[slot])
        copy.start()
        local.append((slot, copy))

    text_f = text_ref[...].astype(F32)
    text_inv = lax.rsqrt(jnp.sum(text_f * text_f, axis=-1, keepdims=True) + EPS)
    texts[0:ROWS, :] = (text_f * text_inv).astype(BF16)

    def to_core(slot):
        send(block(texts, slot), block(texts, 8 + slot), TC + slot, TC + slot, partner)

    def gather_1(ref, base, peer):
        send(block(ref, 0), block(ref, 1), base + 2, base + 2, peer(1))
        send(block(ref, 0), block(ref, 6), base + 0, base + 0, peer(2))
        send(block(ref, 0), block(ref, 2), base + 1, base + 1, peer(6))

    def gather_2(ref, base, peer):
        arrived(block(ref, 1), base + 2)
        send(block(ref, 1), block(ref, 7), base + 3, base + 3, peer(2))
        arrived(block(ref, 2), base + 1)
        send(block(ref, 2), block(ref, 4), base + 4, base + 4, peer(6))
        send(block(ref, 2), block(ref, 3), base + 5, base + 5, peer(1))
        arrived(block(ref, 6), base + 0)

    def piece(ref, slot, start, size):
        return ref.at[pl.ds(slot * ROWS + start, size), :]

    def gather_3(ref, base, peer):
        arrived(block(ref, 7), base + 3)
        send(piece(ref, 7, 0, 48), piece(ref, 5, 0, 48), base + 6, base + 6, peer(2))
        arrived(block(ref, 3), base + 5)
        send(piece(ref, 3, 48, 48), piece(ref, 5, 48, 48), base + 7, base + 7, peer(6))
        arrived(block(ref, 4), base + 4)
        send(piece(ref, 4, 96, 32), piece(ref, 5, 96, 32), base + 8, base + 8, peer(1))

    def gather_4(ref, base):
        arrived(piece(ref, 5, 0, 48), base + 6)
        arrived(piece(ref, 5, 48, 48), base + 7)
        arrived(piece(ref, 5, 96, 32), base + 8)

    to_core(0)

    for slot in SEND_ORDER + [0]:
        for k in (2, 1, 3):
            arrived(part(k, slot), S1 + k * 8 + slot)
        dict(local)[slot].wait()
        if slot:
            send(tile.at[:, pl.ds(slot * ROWS, ROWS)], rows_in.at[MIRROR[slot]],
                 S2 + slot, S2 + MIRROR[slot], image_peer(slot))

    gather_1(texts, TT, text_peer)

    projected = None
    for step, slot in enumerate([0] + [MIRROR[s] for s in SEND_ORDER]):
        if step == 4:
            gather_2(texts, TT, text_peer)
            for s in (1, 2, 6):
                to_core(s)
        for s, copy in proj_copies:
            if s == slot:
                copy.wait()
        if slot == 0:
            features = tile[:, 0:ROWS]
        else:
            arrived(rows_in.at[slot], S2 + slot)
            features = rows_in[slot]
        term = lax.dot_general(features, proj_v[slot], TN, preferred_element_type=F32)
        projected = term if projected is None else projected + term
    image_inv = lax.rsqrt(jnp.sum(projected * projected, axis=-1, keepdims=True) + EPS)
    images[0:ROWS, :] = (projected * image_inv).astype(BF16)
    gather_1(images, IT, image_peer)

    gather_3(texts, TT, text_peer)
    for s in (7, 3, 4):
        to_core(s)
    gather_2(images, IT, image_peer)
    gather_4(texts, TT)
    to_core(5)
    for s in range(8):
        arrived(block(texts, 8 + s), TC + s)

    scale = scale_ref[0]
    slope = -LOG2E * scale
    offset = -LOG2E * bias_ref[0]

    def pair(index, first):
        start = index * 2 * ROWS
        img = images[start:start + 2 * ROWS, :]
        power = slope * lax.dot_general(img, texts[...], NT, preferred_element_type=F32) + offset
        weights[...] = (1.0 / (1.0 + jnp.exp2(power))).astype(BF16)
        if index == 0:
            own = power[0:ROWS, 0:ROWS]
            match = (lax.broadcasted_iota(jnp.int32, (ROWS, ROWS), 0)
                     == lax.broadcasted_iota(jnp.int32, (ROWS, ROWS), 1))
            weights[0:ROWS, 0:ROWS] = jnp.where(
                match, -1.0 / (1.0 + jnp.exp2(-own)), 1.0 / (1.0 + jnp.exp2(own))
            ).astype(BF16)
        grad = scale * jnp.dot(weights[...], texts[...], preferred_element_type=F32)
        img_out[start:start + 2 * ROWS, :] = grad.astype(BF16)
        for slot in (2 * index + 1, 2 * index):
            if slot:
                send(block(img_out, slot), img_in.at[MIRROR[slot]], IR + slot,
                     IR + MIRROR[slot], image_peer(slot))
        term = lax.dot_general(weights[...], img, TN, preferred_element_type=F32)
        if first:
            text_acc[...] = term
        else:
            text_acc[...] += term
        return grad[0:ROWS, :]

    own_grad = pair(0, True)
    gather_3(images, IT, image_peer)
    pair(3, False)
    pair(1, False)
    gather_4(images, IT)
    pair(2, False)

    for s in range(8):
        core_out[s] = text_acc[(8 + s) * ROWS:(9 + s) * ROWS, :].astype(BF16)
        send(core_out.at[s], core_in.at[s], XC + s, XC + s, partner)
    for s in SEND_ORDER:
        arrived(core_in.at[s], XC + s)
        text_out[s] = (text_acc[s * ROWS:(s + 1) * ROWS, :] + core_in[s].astype(F32)).astype(BF16)
        send(text_out.at[s], text_in.at[MIRROR[s]], XR + s, XR + MIRROR[s], text_peer(s))

    grad = own_grad
    for s in range(1, 8):
        arrived(img_in.at[s], IR + s)
        grad = grad + img_in[s].astype(F32)
    unit = images[0:ROWS, :].astype(F32)
    deltas[0:ROWS, :] = (
        (grad - unit * jnp.sum(unit * grad, axis=-1, keepdims=True)) * image_inv
    ).astype(BF16)
    gather_1(deltas, DT, image_peer)
    gather_2(deltas, DT, image_peer)

    def term(index, k):
        cols = slice(index * 2 * ROWS, (index + 1) * 2 * ROWS)
        return jnp.dot(tile[k * FEATS:(k + 1) * FEATS, cols], deltas[cols, :],
                       preferred_element_type=F32)

    for k in range(4):
        gp[k] = term(0, k)
    gather_3(deltas, DT, image_peer)
    for k in range(4):
        gp[k] += term(3, k) + term(1, k)
    gather_4(deltas, DT)
    mine = pl.ds(pl.multiple_of(core * HALF, HALF), HALF)
    other = pl.ds(pl.multiple_of((1 - core) * HALF, HALF), HALF)
    for k in (2, 1, 3, 0):
        gp[k] += term(2, k)
        gp_out[k] = gp[k, :, other].astype(BF16)
        send(gp_out.at[k], gp_in.at[k], GC + k, GC + k, partner)
    for k in (2, 1, 3):
        arrived(gp_in.at[k], GC + k)
        gz_out[k] = (gp[k, :, mine] + gp_in[k].astype(F32)).astype(BF16)
        back = (4 - k) % 4
        send(gz_out.at[k], gz_in.at[back], GZ + k, GZ + back, text_peer(2 * k))
    arrived(gp_in.at[0], GC + 0)

    arrived(core_in.at[0], XC + 0)
    total = text_acc[0:ROWS, :] + core_in[0].astype(F32)
    for s in range(1, 8):
        arrived(text_in.at[s], XR + s)
        total = total + text_in[s].astype(F32)
    total = total * scale
    unit = texts[0:ROWS, :].astype(F32)
    gtext_ref[...] = (total - unit * jnp.sum(unit * total, axis=-1, keepdims=True)) * text_inv

    acc = gp[0, :, mine] + gp_in[0].astype(F32)
    for k in range(1, 4):
        arrived(gz_in.at[k], GZ + k)
        acc = acc + gz_in[k].astype(F32)
    gy_out[...] = acc.astype(BF16)
    send(gy_out, gy_in, GY, GY, across)
    arrived(gy_in, GY)
    gf_out[...] = gy_out[...].astype(F32) + gy_in[...].astype(F32)
    send(gf_out, gf_in, GF, GF, partner)
    gproj_ref[:, mine] = gf_out[...]
    arrived(gf_in, GF)
    gproj_ref[:, other] = gf_in[...]

    for copy in started:
        copy.wait_send()


def on_device(pooled, proj, text, logit_scale, logit_bias):
    vmem = pl.BlockSpec(memory_space=pltpu.VMEM)
    smem = pl.BlockSpec(memory_space=pltpu.SMEM)
    return pl.pallas_call(
        kernel,
        out_shape=(
            jax.ShapeDtypeStruct((ROWS, EMBED), F32),
            jax.ShapeDtypeStruct((FEATS, EMBED), F32),
        ),
        in_specs=[vmem, pl.BlockSpec(memory_space=pl.ANY), vmem, smem, smem],
        out_specs=(vmem, vmem),
        scratch_shapes=[
            pltpu.VMEM((4 * FEATS, 8 * ROWS), BF16),
            pltpu.VMEM((8, 4 * FEATS, ROWS), BF16),
            pltpu.VMEM((8, 4 * FEATS, EMBED), BF16),
            pltpu.VMEM((8 * ROWS, EMBED), BF16),
            pltpu.VMEM((16 * ROWS, EMBED), BF16),
            pltpu.VMEM((16 * ROWS, EMBED), F32),
            pltpu.VMEM((8 * ROWS, EMBED), BF16),
            pltpu.VMEM((8, ROWS, EMBED), BF16),
            pltpu.VMEM((8 * ROWS, EMBED), BF16),
            pltpu.VMEM((8, ROWS, EMBED), BF16),
            pltpu.VMEM((8, ROWS, EMBED), BF16),
            pltpu.VMEM((8, ROWS, EMBED), BF16),
            pltpu.VMEM((8, ROWS, EMBED), BF16),
            pltpu.VMEM((4, FEATS, EMBED), F32),
            pltpu.VMEM((4, FEATS, HALF), BF16),
            pltpu.VMEM((4, FEATS, HALF), BF16),
            pltpu.VMEM((4, FEATS, HALF), BF16),
            pltpu.VMEM((4, FEATS, HALF), BF16),
            pltpu.VMEM((FEATS, HALF), BF16),
            pltpu.VMEM((FEATS, HALF), BF16),
            pltpu.VMEM((FEATS, HALF), F32),
            pltpu.VMEM((FEATS, HALF), F32),
            pltpu.VMEM((2 * ROWS, 16 * ROWS), BF16),
            pltpu.SemaphoreType.DMA((N_SEMS,)),
            pltpu.SemaphoreType.DMA((N_SEMS,)),
            pltpu.SemaphoreType.DMA((8,)),
            pltpu.SemaphoreType.DMA((8, 4)),
        ],
        compiler_params=pltpu.CompilerParams(
            collective_id=0, has_side_effects=True, vmem_limit_bytes=63 * 2**20
        ),
    )(pooled.T, proj, text, logit_scale, logit_bias)


def solution(mesh):
    return jax.shard_map(
        on_device,
        mesh=mesh,
        in_specs=(P("dp", "mp"), P(), P(("dp", "mp"), None), P(), P()),
        out_specs=(P(("dp", "mp"), None), P("mp", None)),
        check_vma=False,
    )
```

time: 713 us -> 136 us (0.19)
  waiting for transfers between devices: 515 us -> 0 us
  Pallas kernels: 0 us -> 130 us
  matrix products: 90.5 us -> 0 us
  starting transfers between devices: 50.7 us -> 0 us
  blocking collectives: 30.6 us -> 0 us
  between operations: 15.3 us -> 1.93 us
    reduce_scatter x1 -> x0, waiting for transfers between devices: 205 us -> none  [on_device(): lax.psum_scatter(image_grad, 'mp', scatter_dimension=0, tiled=True)]
    all_gather x2 -> x0, waiting for transfers between devices: 188 us -> none  [the longest x1 120 us: on_device(): image_unit = lax.all_gather(own_unit, 'mp', axis=0, tiled=True)]
    pallas_call x0 -> x1, Pallas kernels: none -> 130 us  [on_device(): pl.pallas_call(kernel, out_shape=(jax.ShapeDtypeStruct((ROWS, EMBED), F32...]
    dot_general x14 -> x0, matrix products: 90.5 us -> none  [the longest x4 48.6 us: on_device(): jnp.dot(weights, span, preferred_element_type=jnp.float32)]
    psum x1 -> x0, waiting for transfers between devices: 63.9 us -> none  [on_device(): grad_proj = lax.psum(partial_grad, 'dp')]
    ppermute x7 -> x0, waiting for transfers between devices: 58.8 us -> none  [from_behind(): return lax.ppermute(value, axis, pairs)]
    ppermute x7 -> x0, starting transfers between devices: 50.4 us -> none  [from_behind(): return lax.ppermute(value, axis, pairs)]
    all_to_all x1 -> x0, blocking collectives: 30.6 us -> none  [on_device(): lax.all_to_all(pooled, 'mp', split_axis=0, concat_axis=1, tiled=True)]
  transfers between devices with their start and end apart: 11 -> 0, of which waited for: 9 -> 0; matrix products, arithmetic and copies ran while one was open for 8% -> 0% of each run, Pallas kernels for 0% -> 0%
where the time goes in v1:
time: 136 us
  Pallas kernels  130 us (96%)
  local copies, waits for them, and re-layouts  3.97 us (3%)
  between operations  1.93 us (1%)
    pallas_call x1, Pallas kernels, on_device(): pl.pallas_call(kernel, out_shape=(jax.ShapeDtypeStruct((ROWS, EMBED), F32...  130 us
    unnamed x2, local copies, waits for them, and re-layouts  3.97 us

profile of v1, /device:TPU:1, one launch (start us, length us, event | category | flops | bytes accessed | tf_op | source)
XLA Modules:
  0.0 135.5 jit_solution(8961597636897737128)
XLA Ops:
  1.9 129.6 %shard_map.68 = (f32[128,1024]{1,0:T(8,128)}, f32[192,1024]{1,0:T(8,128)}) custom-call(bf16[192,4096]{1,0:T(8,128)(2,1)} %bitcast.1, bf16[6144,1024]{1,0:T(8,128)(2,1)} %proj_ref.1, bf16[128,1024]{1,0:T(8,128)(2,1)} %text_ref.1, f32[1]{0:T(128)S(6)} %copy.9.scale_ref, f32[1]{0:T(128)S(6)} %copy.10.bias_ref), custom_call_target="tpu_custom_call" | custom-call | tf_op jit(solution)/shard_map/pallas_call | solution.py:306
  131.5 1.9 %copy.11 = f32[128,1024]{1,0:T(8,128)} copy(f32[128,1024]{1,0:T(8,128)} %get-tuple-element.4) | data formatting | bytes 1048576
  133.4 2.1 %copy.12 = f32[192,1024]{1,0:T(8,128)} copy(f32[192,1024]{1,0:T(8,128)} %get-tuple-element.5) | data formatting | bytes 1572864

commit v2 on v1

v2 whole, which is shorter than its diff:
```python
import functools

import jax
import jax.numpy as jnp
from jax import lax
from jax.experimental import pallas as pl
from jax.experimental.pallas import tpu as pltpu
from jax.sharding import PartitionSpec as P

EPS = 1e-06
LOG2E = 1.4426950408889634
MESH = pl.DeviceIdType.MESH
F32 = jnp.float32
BF16 = jnp.bfloat16
NT = (((1,), (1,)), ((), ()))
TN = (((0,), (0,)), ((), ()))
ROWS = 128
FEATS = 192
EMBED = 1024
HALF = EMBED // 2
QUARTER = EMBED // 4
OFFSETS = [(0, 0), (0, 1), (1, 0), (3, 0), (1, 1), (3, 1), (2, 0), (2, 1)]
MIRROR = [0, 1, 3, 2, 5, 4, 6, 7]
SEND_ORDER = [7,6,4,5,1,2,3]
BESIDE, NEXT, BACK = 1, 2, 3
AHEAD = 8
LAG = 4


def sems(*sizes):
    bases, total = [], 0
    for size in sizes:
        bases.append(total)
        total += size
    return bases, total


(S1, S2, TT, TC, IT, IR, DT, XC, XR, GC, GZ, GY, GF), N_SEMS = sems(
    32, 8, 9, 8, 9, 9, 18, 8, 9, 8, 8, 2, 2
)


def kernel(
    pooled_ref, proj_ref, text_ref, scale_ref, bias_ref, gtext_ref, gproj_ref,
    tile, rows_in, proj_v, images, texts, text_acc, img_out, img_in, deltas,
    core_out, core_in, text_out, text_in, gp, gp_out, gp_in, gz_out, gz_in,
    gy_out, gy_in, gf_out, gf_in, weights, send_sem, recv_sem, local_sem, proj_sem,
):
    dp = lax.axis_index("dp")
    mp = lax.axis_index("mp")
    core = dp % 2
    y = (dp // 2) * 2 + (mp // 4) % 2
    x = mp % 4
    z = mp // 8
    y_a = y + 1 - 2 * (y % 2)
    y_b = 3 - y

    def device(x_, y_, z_, core_):
        return ((y_ // 2) * 2 + core_, (z_ * 2 + y_ % 2) * 4 + x_)

    def image_peer(slot):
        steps, beside = OFFSETS[slot]
        return device((x + steps) % 4, y_a if beside else y, z, core)

    def text_peer(slot):
        steps, beside = OFFSETS[slot]
        return device(x, y_b if beside else y, (z + steps) % 4, core)

    def ring_peer(steps):
        return device(x, y, (z + steps) % 4, core)

    partner = device(x, y, z, 1 - core)
    across = device(x, (y + 2) % 4, z, core)

    def position(slot):
        steps, beside = OFFSETS[slot]
        return (y_a if beside else y) % 2 * 4 + (x + steps) % 4

    started = []

    def send(src, dst, sem_out, sem_in, to):
        copy = pltpu.make_async_remote_copy(
            src_ref=src, dst_ref=dst, send_sem=send_sem.at[sem_out],
            recv_sem=recv_sem.at[sem_in], device_id=to, device_id_type=MESH,
        )
        copy.start()
        started.append(copy)

    def arrived(dst, sem):
        pltpu.make_async_copy(dst, dst, recv_sem.at[sem]).wait()

    barrier = pltpu.get_barrier_semaphore()
    peers = [image_peer(s) for s in range(1, 8)] + [text_peer(s) for s in range(1, 8)]
    peers += [partner, across]
    for peer in peers:
        pl.semaphore_signal(barrier, inc=1, device_id=peer, device_id_type=MESH)

    whole = slice(None)

    def block(ref, slot, cols=whole):
        return ref.at[pl.ds(slot * ROWS, ROWS), cols]

    def part(k, slot):
        return tile.at[pl.ds(k * FEATS, FEATS), pl.ds(slot * ROWS, ROWS)]

    def shard_columns(dz, slot):
        start = (z + dz) % 4 * 1024 + position(slot) * ROWS
        return pooled_ref.at[:, pl.ds(pl.multiple_of(start, ROWS), ROWS)]

    pl.semaphore_wait(barrier, len(peers))

    order = SEND_ORDER + [0]
    local = {}

    def first_stage(slot):
        for dz in (2, 1, 3):
            k = (4 - dz) % 4
            send(shard_columns(dz, slot), part(k, slot), S1 + dz * 8 + slot,
                 S1 + k * 8 + slot, ring_peer(dz))
        local[slot] = pltpu.make_async_copy(
            shard_columns(0, slot), part(0, slot), local_sem.at[slot])
        local[slot].start()

    for slot in order[:AHEAD]:
        first_stage(slot)

    proj_copies = []
    for slot in [MIRROR[s] for s in SEND_ORDER] + [0]:
        for k in range(4):
            shard = (z + k) % 4 * 8 + position(slot)
            copy = pltpu.make_async_copy(
                proj_ref.at[pl.ds(pl.multiple_of(shard * FEATS, FEATS), FEATS), :],
                proj_v.at[slot, pl.ds(k * FEATS, FEATS), :],
                proj_sem.at[slot, k],
            )
            copy.start()
            proj_copies.append((slot, copy))

    text_f = text_ref[...].astype(F32)
    text_inv = lax.rsqrt(jnp.sum(text_f * text_f, axis=-1, keepdims=True) + EPS)
    texts[0:ROWS, :] = (text_f * text_inv).astype(BF16)

    def to_core(slot):
        send(block(texts, slot), block(texts, 8 + slot), TC + slot, TC + slot, partner)

    def piece(ref, slot, start, size, cols=whole):
        return ref.at[pl.ds(slot * ROWS + start, size), cols]

    def gather_1(ref, base, peer, cols=whole):
        send(block(ref, 0, cols), block(ref, 1, cols), base + 0, base + 0, peer(BESIDE))
        send(block(ref, 0, cols), block(ref, 3, cols), base + 1, base + 1, peer(NEXT))
        send(block(ref, 0, cols), block(ref, 2, cols), base + 2, base + 2, peer(BACK))

    def gather_2(ref, base, peer, cols=whole):
        arrived(block(ref, 1, cols), base + 0)
        send(block(ref, 1, cols), block(ref, 5, cols), base + 3, base + 3, peer(NEXT))
        arrived(block(ref, 2, cols), base + 2)
        send(block(ref, 2, cols), block(ref, 6, cols), base + 4, base + 4, peer(BACK))
        send(block(ref, 2, cols), block(ref, 4, cols), base + 5, base + 5, peer(BESIDE))
        arrived(block(ref, 3, cols), base + 1)

    def gather_3(ref, base, peer, cols=whole):
        arrived(block(ref, 5, cols), base + 3)
        send(piece(ref, 5, 0, 48, cols), piece(ref, 7, 0, 48, cols), base + 6, base + 6, peer(NEXT))
        arrived(block(ref, 4, cols), base + 5)
        send(piece(ref, 4, 48, 48, cols), piece(ref, 7, 48, 48, cols), base + 7, base + 7, peer(BACK))
        arrived(block(ref, 6, cols), base + 4)
        send(piece(ref, 6, 96, 32, cols), piece(ref, 7, 96, 32, cols), base + 8, base + 8, peer(BESIDE))

    def gather_4(ref, base, cols=whole):
        arrived(piece(ref, 7, 0, 48, cols), base + 6)
        arrived(piece(ref, 7, 48, 48, cols), base + 7)
        arrived(piece(ref, 7, 96, 32, cols), base + 8)

    def reduce_1(ref, ref_in, base, peer):
        send(piece(ref, 7, 0, 48), piece(ref_in, 7, 0, 48), base + 6, base + 6, peer(BACK))
        send(piece(ref, 7, 48, 48), piece(ref_in, 7, 48, 48), base + 7, base + 7, peer(NEXT))
        send(piece(ref, 7, 96, 32), piece(ref_in, 7, 96, 32), base + 8, base + 8, peer(BESIDE))

    def reduce_2(slot, ref, ref_in, base, peer, own):
        start, size, sem, at, towards = {
            5: (0, 48, 6, 3, BACK), 4: (48, 48, 7, 5, BESIDE), 6: (96, 32, 8, 4, NEXT)
        }[slot]
        arrived(piece(ref_in, 7, start, size), base + sem)
        ref[slot * ROWS:(slot + 1) * ROWS, :] = own(slot).astype(BF16)
        rows = slice(slot * ROWS + start, slot * ROWS + start + size)
        part_in = ref_in[7 * ROWS + start:7 * ROWS + start + size, :].astype(F32)
        ref[rows, :] = (own(slot)[start:start + size, :] + part_in).astype(BF16)
        send(block(ref, slot), block(ref_in, slot), base + at, base + at, peer(towards))

    def reduce_3(slot, ref, ref_in, base, peer, own):
        total = own(slot)
        for at, sem in {1: [(5, 3)], 2: [(6, 4), (4, 5)], 3: []}[slot]:
            arrived(block(ref_in, at), base + sem)
            total = total + ref_in[at * ROWS:(at + 1) * ROWS, :].astype(F32)
        ref[slot * ROWS:(slot + 1) * ROWS, :] = total.astype(BF16)
        send(block(ref, slot), block(ref_in, slot), base + slot - 1, base + slot - 1, peer(slot))

    def reduce_4(total, ref_in, base):
        for slot in (1, 2, 3):
            arrived(block(ref_in, slot), base + slot - 1)
            total = total + ref_in[slot * ROWS:(slot + 1) * ROWS, :].astype(F32)
        return total

    to_core(0)

    def project(slot):
        for s, copy in proj_copies:
            if s == slot:
                copy.wait()
        if slot:
            arrived(rows_in.at[slot], S2 + slot)
        features = rows_in[slot] if slot else tile[:, 0:ROWS]
        return lax.dot_general(features, proj_v[slot], TN, preferred_element_type=F32)

    projected = jnp.zeros((ROWS, EMBED), F32)
    for step, slot in enumerate(order):
        for k in (2, 1, 3):
            arrived(part(k, slot), S1 + k * 8 + slot)
        local[slot].wait()
        if step + AHEAD < 8:
            first_stage(order[step + AHEAD])
        if slot:
            send(tile.at[:, pl.ds(slot * ROWS, ROWS)], rows_in.at[MIRROR[slot]],
                 S2 + slot, S2 + MIRROR[slot], image_peer(slot))
        if step >= LAG:
            projected = projected + project(MIRROR[order[step - LAG]])
        if step == 5:
            gather_1(texts, TT, text_peer)
    projected = projected + project(0)
    for slot in order[8 - LAG:7]:
        projected = projected + project(MIRROR[slot])
        if slot == order[5]:
            gather_2(texts, TT, text_peer)
            for s in (1, 2, 3):
                to_core(s)
    image_inv = lax.rsqrt(jnp.sum(projected * projected, axis=-1, keepdims=True) + EPS)
    images[0:ROWS, :] = (projected * image_inv).astype(BF16)
    gather_1(images, IT, image_peer)

    gather_3(texts, TT, text_peer)
    for s in (4, 5, 6):
        to_core(s)
    gather_2(images, IT, image_peer)
    gather_4(texts, TT)
    to_core(7)
    for s in range(8):
        arrived(block(texts, 8 + s), TC + s)

    scale = scale_ref[0]
    slope = -LOG2E * scale
    offset = -LOG2E * bias_ref[0]

    def pair(index):
        start = index * 2 * ROWS
        rows = slice(start, start + 2 * ROWS)
        power = slope * lax.dot_general(
            images[rows, :], texts[...], NT, preferred_element_type=F32) + offset
        weights[rows, :] = (1.0 / (1.0 + jnp.exp2(power))).astype(BF16)
        if index == 0:
            own = power[0:ROWS, 0:ROWS]
            match = (lax.broadcasted_iota(jnp.int32, (ROWS, ROWS), 0)
                     == lax.broadcasted_iota(jnp.int32, (ROWS, ROWS), 1))
            weights[0:ROWS, 0:ROWS] = jnp.where(
                match, -1.0 / (1.0 + jnp.exp2(-own)), 1.0 / (1.0 + jnp.exp2(own))
            ).astype(BF16)
        grad = jnp.dot(weights[rows, :], texts[...], preferred_element_type=F32)
        img_out[rows, :] = grad.astype(BF16)
        return grad[0:ROWS, :]

    def text_term(first, last):
        rows = slice(first * 2 * ROWS, (last + 1) * 2 * ROWS)
        return lax.dot_general(
            weights[rows, :], images[rows, :], TN, preferred_element_type=F32)

    def image_part(slot):
        return img_out[slot * ROWS:(slot + 1) * ROWS, :].astype(F32)

    images_tree = (img_out, img_in, IR, image_peer, image_part)
    own_grad = pair(0)
    gather_3(images, IT, image_peer)
    pair(1)
    text_acc[...] = text_term(0, 1)
    gather_4(images, IT)
    pair(3)
    reduce_1(img_out, img_in, IR, image_peer)
    pair(2)
    for s in (5, 4, 6):
        reduce_2(s, *images_tree)
    reduce_3(3, *images_tree)
    text_acc[...] += text_term(2, 3)

    for s in (7, 5, 4, 6, 1, 2, 3, 0):
        core_out[s] = text_acc[(8 + s) * ROWS:(9 + s) * ROWS, :].astype(BF16)
        send(core_out.at[s], core_in.at[s], XC + s, XC + s, partner)

    def text_part(slot):
        return text_acc[slot * ROWS:(slot + 1) * ROWS, :] + core_in[slot].astype(F32)

    texts_tree = (text_out, text_in, XR, text_peer, text_part)
    reduce_3(1, *images_tree)
    reduce_3(2, *images_tree)
    arrived(core_in.at[7], XC + 7)
    text_out[7 * ROWS:8 * ROWS, :] = text_part(7).astype(BF16)
    reduce_1(text_out, text_in, XR, text_peer)
    for s in (5, 4, 6):
        arrived(core_in.at[s], XC + s)
        reduce_2(s, *texts_tree)
    arrived(core_in.at[3], XC + 3)
    reduce_3(3, *texts_tree)

    grad = reduce_4(own_grad, img_in, IR)
    unit = images[0:ROWS, :].astype(F32)
    deltas[0:ROWS, :] = (
        (grad - unit * jnp.sum(unit * grad, axis=-1, keepdims=True)) * image_inv
    ).astype(BF16)
    cols = [pl.ds(0, HALF), pl.ds(HALF, HALF)]
    mine = pl.ds(pl.multiple_of(core * QUARTER, QUARTER), QUARTER)
    other = pl.ds(pl.multiple_of((1 - core) * QUARTER, QUARTER), QUARTER)

    def place(half, which):
        return pl.ds(pl.multiple_of(half * HALF + which * QUARTER, QUARTER), QUARTER)

    def multiply(h):
        for k in (2, 1, 3, 0):
            gp[h, k] = jnp.dot(tile[k * FEATS:(k + 1) * FEATS, :], deltas[:, h * HALF:(h + 1) * HALF],
                               preferred_element_type=F32)
            gp_out[h, k] = gp[h, k, :, other].astype(BF16)
            send(gp_out.at[h, k], gp_in.at[h, k], GC + 4 * h + k, GC + 4 * h + k, partner)

    def along_z(h):
        for k in (2, 1, 3):
            arrived(gp_in.at[h, k], GC + 4 * h + k)
            gz_out[h, k] = (gp[h, k, :, mine] + gp_in[h, k].astype(F32)).astype(BF16)
            back = (4 - k) % 4
            send(gz_out.at[h, k], gz_in.at[h, back], GZ + 4 * h + k, GZ + 4 * h + back, ring_peer(k))

    def along_y(h):
        arrived(gp_in.at[h, 0], GC + 4 * h)
        acc = gp[h, 0, :, mine] + gp_in[h, 0].astype(F32)
        for k in range(1, 4):
            arrived(gz_in.at[h, k], GZ + 4 * h + k)
            acc = acc + gz_in[h, k].astype(F32)
        gy_out[h] = acc.astype(BF16)
        send(gy_out.at[h], gy_in.at[h], GY + h, GY + h, across)

    def to_partner(h):
        arrived(gy_in.at[h], GY + h)
        gf_out[h] = gy_out[h].astype(F32) + gy_in[h].astype(F32)
        send(gf_out.at[h], gf_in.at[h], GF + h, GF + h, partner)
        gproj_ref[:, place(h, core)] = gf_out[h]

    def finish(h):
        arrived(gf_in.at[h], GF + h)
        gproj_ref[:, place(h, 1 - core)] = gf_in[h]

    gather_1(deltas, DT, image_peer, cols[0])
    for s in (1, 2):
        arrived(core_in.at[s], XC + s)
        reduce_3(s, *texts_tree)
    gather_2(deltas, DT, image_peer, cols[0])
    gather_1(deltas, DT + 9, image_peer, cols[1])
    gather_3(deltas, DT, image_peer, cols[0])
    gather_2(deltas, DT + 9, image_peer, cols[1])
    gather_4(deltas, DT, cols[0])
    multiply(0)
    gather_3(deltas, DT + 9, image_peer, cols[1])
    along_z(0)
    gather_4(deltas, DT + 9, cols[1])
    multiply(1)
    along_y(0)
    along_z(1)

    arrived(core_in.at[0], XC + 0)
    total = reduce_4(text_part(0), text_in, XR)
    unit = texts[0:ROWS, :].astype(F32)
    gtext_ref[...] = (total - unit * jnp.sum(unit * total, axis=-1, keepdims=True)) * text_inv
    to_partner(0)
    along_y(1)
    finish(0)
    to_partner(1)
    finish(1)

    for copy in started:
        copy.wait_send()


def on_device(pooled, proj, text, logit_scale, logit_bias):
    vmem = pl.BlockSpec(memory_space=pltpu.VMEM)
    smem = pl.BlockSpec(memory_space=pltpu.SMEM)
    grad_text, grad_proj = pl.pallas_call(
        kernel,
        out_shape=(
            jax.ShapeDtypeStruct((ROWS, EMBED), F32),
            jax.ShapeDtypeStruct((FEATS, EMBED), F32),
        ),
        in_specs=[vmem, pl.BlockSpec(memory_space=pl.ANY), vmem, smem, smem],
        out_specs=(vmem, vmem),
        scratch_shapes=[
            pltpu.VMEM((4 * FEATS, 8 * ROWS), BF16),
            pltpu.VMEM((8, 4 * FEATS, ROWS), BF16),
            pltpu.VMEM((8, 4 * FEATS, EMBED), BF16),
            pltpu.VMEM((8 * ROWS, EMBED), BF16),
            pltpu.VMEM((16 * ROWS, EMBED), BF16),
            pltpu.VMEM((16 * ROWS, EMBED), F32),
            pltpu.VMEM((8 * ROWS, EMBED), BF16),
            pltpu.VMEM((8 * ROWS, EMBED), BF16),
            pltpu.VMEM((8 * ROWS, EMBED), BF16),
            pltpu.VMEM((8, ROWS, EMBED), BF16),
            pltpu.VMEM((8, ROWS, EMBED), BF16),
            pltpu.VMEM((8 * ROWS, EMBED), BF16),
            pltpu.VMEM((8 * ROWS, EMBED), BF16),
            pltpu.VMEM((2, 4, FEATS, HALF), F32),
            pltpu.VMEM((2, 4, FEATS, QUARTER), BF16),
            pltpu.VMEM((2, 4, FEATS, QUARTER), BF16),
            pltpu.VMEM((2, 4, FEATS, QUARTER), BF16),
            pltpu.VMEM((2, 4, FEATS, QUARTER), BF16),
            pltpu.VMEM((2, FEATS, QUARTER), BF16),
            pltpu.VMEM((2, FEATS, QUARTER), BF16),
            pltpu.VMEM((2, FEATS, QUARTER), F32),
            pltpu.VMEM((2, FEATS, QUARTER), F32),
            pltpu.VMEM((8 * ROWS, 16 * ROWS), BF16),
            pltpu.SemaphoreType.DMA((N_SEMS,)),
            pltpu.SemaphoreType.DMA((N_SEMS,)),
            pltpu.SemaphoreType.DMA((8,)),
            pltpu.SemaphoreType.DMA((8, 4)),
        ],
        compiler_params=pltpu.CompilerParams(
            collective_id=0, has_side_effects=True, vmem_limit_bytes=63 * 2**20
        ),
    )(pooled.T, proj, text, logit_scale, logit_bias)
    return (logit_scale[0] * grad_text, logit_scale[0] * grad_proj)


def solution(mesh):
    return jax.shard_map(
        on_device,
        mesh=mesh,
        in_specs=(P("dp", "mp"), P(), P(("dp", "mp"), None), P(), P()),
        out_specs=(P(("dp", "mp"), None), P("mp", None)),
        check_vma=False,
    )
```

time: 136 us -> 123 us (0.904)
  Pallas kernels: 130 us -> 117 us
  other arithmetic: 0 us -> 3.99 us
  local copies, waits for them, and re-layouts: 3.97 us -> 0 us
    pallas_call x1, Pallas kernels: 130 us -> 117 us  [on_device(): pl.pallas_call(kernel, out_shape=(jax.ShapeDtypeStruct((ROWS, EMBED), F32...]
    mul x0 -> x2, other arithmetic: none -> 3.99 us  [on_device(): return (logit_scale[0] * grad_text, logit_scale[0] * grad_proj)]
    unnamed x2 -> x0, local copies, waits for them, and re-layouts: 3.97 us -> none
where the time goes in v2:
time: 123 us
  Pallas kernels  117 us (95%)
  other arithmetic  3.99 us (3%)
  between operations  1.93 us (2%)
    pallas_call x1, Pallas kernels, on_device(): pl.pallas_call(kernel, out_shape=(jax.ShapeDtypeStruct((ROWS, EMBED), F32...  117 us
    mul x2, other arithmetic, on_device(): return (logit_scale[0] * grad_text, logit_scale[0] * grad_proj)  3.99 us

profile of v2, /device:TPU:1, one launch (start us, length us, event | category | flops | bytes accessed | tf_op | source)
XLA Modules:
  0.0 122.9 jit_solution(16143911190068902535)
XLA Ops:
  1.9 117.0 %shard_map.68 = (f32[128,1024]{1,0:T(8,128)}, f32[192,1024]{1,0:T(8,128)}) custom-call(bf16[192,4096]{1,0:T(8,128)(2,1)} %bitcast.4, bf16[6144,1024]{1,0:T(8,128)(2,1)} %proj_ref.1, bf16[128,1024]{1,0:T(8,128)(2,1)} %text_ref.1, f32[1]{0:T(128)} %copy.7.scale_ref, f32[1]{0:T(128)S(6)} %copy.8.bias_ref), custom_call_target="tpu_custom_call" | custom-call | tf_op jit(solution)/shard_map/pallas_call | solution.py:391
  118.9 1.9 %broadcast_multiply_fusion.1 = f32[128,1024]{1,0:T(8,128)} fusion(f32[128,1024]{1,0:T(8,128)} %get-tuple-element.4, f32[]{:T(128)} %bitcast.2), kind=kLoop, calls=%fused_computation.1 | loop fusion | flops 131072 | bytes 1048580 | tf_op jit(solution)/shard_map/mul | solution.py:432
  120.8 2.1 %broadcast_multiply_fusion = f32[192,1024]{1,0:T(8,128)} fusion(f32[192,1024]{1,0:T(8,128)} %get-tuple-element.5, f32[]{:T(128)} %bitcast.3), kind=kLoop, calls=%fused_computation | loop fusion | flops 196608 | bytes 1572868 | tf_op jit(solution)/shard_map/mul | solution.py:432

commit v3 on v2

--- a/solution.py
+++ b/solution.py
@@ -202,8 +202,6 @@
             total = total + ref_in[slot * ROWS:(slot + 1) * ROWS, :].astype(F32)
         return total
 
-    to_core(0)
-
     def project(slot):
         for s, copy in proj_copies:
             if s == slot:
@@ -227,6 +225,7 @@
             projected = projected + project(MIRROR[order[step - LAG]])
         if step == 5:
             gather_1(texts, TT, text_peer)
+            to_core(0)
     projected = projected + project(0)
     for slot in order[8 - LAG:7]:
         projected = projected + project(MIRROR[slot])
@@ -278,17 +277,17 @@
 
     images_tree = (img_out, img_in, IR, image_peer, image_part)
     own_grad = pair(0)
-    gather_3(images, IT, image_peer)
     pair(1)
     text_acc[...] = text_term(0, 1)
+    gather_3(images, IT, image_peer)
+    pair(2)
     gather_4(images, IT)
     pair(3)
     reduce_1(img_out, img_in, IR, image_peer)
-    pair(2)
+    text_acc[...] += text_term(2, 3)
     for s in (5, 4, 6):
         reduce_2(s, *images_tree)
     reduce_3(3, *images_tree)
-    text_acc[...] += text_term(2, 3)
 
     for s in (7, 5, 4, 6, 1, 2, 3, 0):
         core_out[s] = text_acc[(8 + s) * ROWS:(9 + s) * ROWS, :].astype(BF16)

time: 123 us -> 126 us (1.024)
  Pallas kernels: 117 us -> 120 us
    pallas_call x1, Pallas kernels: 117 us -> 120 us  [on_device(): pl.pallas_call(kernel, out_shape=(jax.ShapeDtypeStruct((ROWS, EMBED), F32...]
where the time goes in v3:
time: 126 us
  Pallas kernels  120 us (95%)
  other arithmetic  3.99 us (3%)
  between operations  1.93 us (2%)
    pallas_call x1, Pallas kernels, on_device(): pl.pallas_call(kernel, out_shape=(jax.ShapeDtypeStruct((ROWS, EMBED), F32...  120 us
    mul x2, other arithmetic, on_device(): return (logit_scale[0] * grad_text, logit_scale[0] * grad_proj)  3.99 us

profile of v3, /device:TPU:1, one launch (start us, length us, event | category | flops | bytes accessed | tf_op | source)
XLA Modules:
  0.0 126.2 jit_solution(11017331689362620636)
XLA Ops:
  1.9 120.3 %shard_map.68 = (f32[128,1024]{1,0:T(8,128)}, f32[192,1024]{1,0:T(8,128)}) custom-call(bf16[192,4096]{1,0:T(8,128)(2,1)} %bitcast.4, bf16[6144,1024]{1,0:T(8,128)(2,1)} %proj_ref.1, bf16[128,1024]{1,0:T(8,128)(2,1)} %text_ref.1, f32[1]{0:T(128)} %copy.7.scale_ref, f32[1]{0:T(128)S(6)} %copy.8.bias_ref), custom_call_target="tpu_custom_call" | custom-call | tf_op jit(solution)/shard_map/pallas_call | solution.py:390
  122.2 1.9 %broadcast_multiply_fusion.1 = f32[128,1024]{1,0:T(8,128)} fusion(f32[128,1024]{1,0:T(8,128)} %get-tuple-element.4, f32[]{:T(128)} %bitcast.2), kind=kLoop, calls=%fused_computation.1 | loop fusion | flops 131072 | bytes 1048580 | tf_op jit(solution)/shard_map/mul | solution.py:431
  124.1 2.1 %broadcast_multiply_fusion = f32[192,1024]{1,0:T(8,128)} fusion(f32[192,1024]{1,0:T(8,128)} %get-tuple-element.5, f32[]{:T(128)} %bitcast.3), kind=kLoop, calls=%fused_computation | loop fusion | flops 196608 | bytes 1572868 | tf_op jit(solution)/shard_map/mul | solution.py:431
